TPU v7x, 256 devices: a whole 4x4x8 slice. The times are simulated.
256 devices in a mesh: dp: 16 (over x, y_lo, core), mp: 16 (over z, y_hi).
Axes of the slice: x: 4, y: 4 (y_hi: 2, y_lo: 2; y = y_hi * 2 + y_lo), z: 8, core: 2. Of those that a mesh axis runs over, the one named last changes fastest.
Arguments:
- grads: bfloat16 [16, 64, 512, 512], P('dp', 'mp'), may hold values from -150 to 150, as said below
- owners: int32 [128, 1], P('mp'), may hold values from 0 to 15; in each aligned block of 8 rows (0 to 7, 8 to 15, ...) at most 2 rows name the same one
- roots_prev: bfloat16 [64, 2, 512, 512], P('mp'), may hold values from -1 to 3, as said below
- moment_first: float32 [64, 512, 512], P('mp', 'dp'), may hold values from -1.8 to 1.8
- moment_second: float32 [64, 512, 512], P('mp', 'dp'), may hold values from 0.01 to 1
Outputs:
- update: float32 [64, 512, 512], P('mp', 'dp')
- moment_first_new: float32 [64, 512, 512], P('mp', 'dp')
- moment_second_new: float32 [64, 512, 512], P('mp', 'dp')
- roots_new: bfloat16 [16, 16, 2, 512, 512], P('dp', 'mp')
Inputs may be any that keep to these rules, and one draw needn't show every extreme that they name: `owners`: in the 8 statistics of one index of mp no index of dp is named more than 2 times, and one is named exactly 2 times. `grads`: independent entries. `roots_prev`: each matrix is symmetric.
All inputs are finite; a program needn't handle non-finite values.
Results may differ from a plain program's by a relative error of at most 0.001.
The roundings to bfloat16 on the way count: a program that leaves them out, or rounds other values in their place, can miss the bound.
Values may be sent and summed in bfloat16 or wider, within the bound.
A program may use at most 128 MiB of HBM per device.

v0:
```python
import jax
import jax.numpy as jnp
from jax import lax
from jax.sharding import PartitionSpec as P

CAP = 2
ITERS = 3


HIGHEST_PRECISION = lax.Precision.HIGHEST


def count_before(labels):
    total_items = labels.shape[0]
    matches = labels[:, None] == labels[None, :]
    row_ids = lax.broadcasted_iota(jnp.int32, (total_items, total_items), 0)
    col_ids = lax.broadcasted_iota(jnp.int32, (total_items, total_items), 1)
    return jnp.sum(jnp.where(matches & (col_ids < row_ids), 1, 0), axis=1).astype(jnp.int32)


def inverse_root(statistic):
    block_order = statistic.shape[-1]
    identity = jnp.eye(block_order, dtype=statistic.dtype)
    shifted = statistic + 0.0001 * identity
    norm_value = jnp.sqrt(jnp.sum(shifted * shifted))
    coupled = shifted / norm_value
    iterate = identity
    for step_id in range(ITERS):
        factor = (5.0 * identity - coupled) / 4.0
        if step_id == 0:
            iterate = factor
        else:
            iterate = jnp.dot(iterate, factor, precision=HIGHEST_PRECISION)
        if step_id + 1 < ITERS:
            factor_sq = jnp.dot(factor, factor, precision=HIGHEST_PRECISION)
            factor_quad = jnp.dot(factor_sq, factor_sq, precision=HIGHEST_PRECISION)
            coupled = jnp.dot(factor_quad, coupled, precision=HIGHEST_PRECISION)
    return iterate


def per_device(grads, owners, roots_prev, moment_first, moment_second):
    data_count = lax.axis_size("dp")
    my_index = lax.axis_index("dp")
    local_grads = grads[0]
    block_order = local_grads.shape[1]
    row_count = block_order // data_count
    left_part = jnp.einsum(
        "bik,bjk->bij", local_grads, local_grads, preferred_element_type=jnp.float32
    )
    right_part = jnp.einsum(
        "bki,bkj->bij", local_grads, local_grads, preferred_element_type=jnp.float32
    )
    left_mine = lax.dynamic_slice_in_dim(roots_prev[:, 0], my_index * row_count, row_count, 1)
    left_rows, right_rows = (
        lax.psum_scatter(left_part, "dp", scatter_dimension=1, tiled=True),
        lax.psum_scatter(right_part, "dp", scatter_dimension=1, tiled=True),
    )
    grad_whole = lax.psum(local_grads.astype(jnp.float32), "dp") / data_count
    grad_rows = lax.dynamic_slice_in_dim(grad_whole, my_index * row_count, row_count, 1)
    product = jnp.einsum(
        "bij,bjk->bik",
        left_mine,
        grad_whole.astype(jnp.bfloat16),
        preferred_element_type=jnp.float32,
    )
    left_rows = left_rows / data_count
    right_rows = right_rows / data_count
    sectioned = product.astype(jnp.bfloat16)
    precond = jnp.einsum(
        "bij,bjk->bik", sectioned, roots_prev[:, 1], preferred_element_type=jnp.float32
    )
    first_new = 0.9 * moment_first + 0.1 * grad_rows
    second_new = 0.95 * moment_second + 0.05 * grad_rows * grad_rows
    adam_step = first_new / (jnp.sqrt(second_new) + 1e-08)
    square_sums = lax.psum(
        (jnp.sum(adam_step * adam_step), jnp.sum(precond * precond)), ("dp", "mp")
    )
    graft_ratio = jnp.sqrt(square_sums[0]) / jnp.sqrt(square_sums[1] + 1e-06)
    owner_ids = owners[:, 0]
    mats = owner_ids.shape[0]
    owner_slot = count_before(owner_ids)
    stacked = jnp.stack((left_rows, right_rows), axis=1).reshape(mats, row_count, block_order)
    slot_count = CAP
    choose = (
        owner_ids[None, None, :] == lax.broadcasted_iota(jnp.int32, (slot_count, data_count, 1), 1)
    ) & (
        owner_slot[None, None, :] == lax.broadcasted_iota(jnp.int32, (slot_count, data_count, 1), 0)
    )
    outgoing = jnp.einsum(
        "koi,irs->kors", choose.astype(jnp.float32), stacked, precision=HIGHEST_PRECISION
    )
    received = lax.all_to_all(outgoing, "dp", split_axis=1, concat_axis=1, tiled=True)
    item_count = received.shape[0]
    assembled = received.reshape(item_count, data_count * row_count, block_order)
    solved = jax.vmap(inverse_root)(assembled).astype(jnp.bfloat16)
    slot_range = lax.broadcasted_iota(jnp.int32, (CAP, 1), 0)
    mine = (owner_ids[None, :] == my_index) & (owner_slot[None, :] == slot_range)
    filled = jnp.any(mine, axis=1)
    roots_new = jnp.where(filled[:, None, None], solved, jnp.zeros_like(solved))
    return (graft_ratio * precond, first_new, second_new, roots_new[None, None])


def solution(mesh):
    return jax.shard_map(
        per_device,
        mesh=mesh,
        in_specs=(
            P("dp", "mp", None, None),
            P("mp", None),
            P("mp", None, None, None),
            P("mp", "dp", None),
            P("mp", "dp", None),
        ),
        out_specs=(
            P("mp", "dp", None),
            P("mp", "dp", None),
            P("mp", "dp", None),
            P("dp", "mp", None, None, None),
        ),
        check_vma=False,
    )
```

profile of v0, /device:TPU:1, one launch (start us, length us, event | category | flops | bytes accessed | tf_op | source)
XLA Modules:
  0.0 444.3 jit_solution(10740983080634684644)
XLA Ops:
  7.2 5.5 %fusion.3 = f32[4,512,512]{2,1,0:T(8,128)} fusion(bf16[1,4,512,512]{3,2,1,0:T(8,128)(2,1)} %param.5), kind=kOutput, calls=%fused_computation.4 | convolution fusion | flops 1073741824 | bytes 6291456 | tf_op jit(solution)/shard_map/bki,bkj->bij/dot_general | solution.py:50
  12.8 1.5 copy-done
  14.3 3.2 fusion.5
  17.6 2.6 bitcast_convert_fusion
  20.2 0.6 copy-done.4
  21.0 62.5 %reduce-scatter.5.cloned.1.call-done = f32[4,32,512]{2,1,0:T(8,128)} async-done(((f32[4,512,512]{2,1,0:T(8,128)}), f32[4,32,512]{2,1,0:T(8,128)}) %reduce-scatter.5.cloned.1.call-update) | async-done | bytes 262160 | tf_op jit(solution)/shard_map/reduce_scatter | solution.py:56
  83.5 1.0 multiply_bitcast_fusion
  84.5 70.3 %reduce-scatter.3.cloned.1.call-done = f32[4,32,512]{2,1,0:T(8,128)} async-done(((f32[4,512,512]{2,1,0:T(8,128)}), f32[4,32,512]{2,1,0:T(8,128)}) %reduce-scatter.3.cloned.1.call-update) | async-done | bytes 262160 | tf_op jit(solution)/shard_map/reduce_scatter | solution.py:55
  154.8 1.0 multiply_bitcast_fusion.1
  155.9 1.1 fusion.41
  157.0 2.6 copy.26
  159.6 7.3 %all-to-all-start = ((f32[2,16,32,512]{3,2,0,1:T(8,128)}), f32[2,16,32,512]{3,2,0,1:T(8,128)S(1)}, u32[]{:S(2)}, u32[]{:S(2)}) async-start(f32[2,16,32,512]{3,2,0,1:T(8,128)} %copy.26), calls=%async_computation.2 | async-start | bytes 4194304 | tf_op jit(solution)/shard_map/all_to_all | solution.py:92
  167.1 3.0 slice.6
  170.1 1.2 fusion.38
  171.4 1.1 fusion.40
  172.5 141.4 %all-reduce.3.cloned.1.call-done = f32[4,512,512]{2,1,0:T(8,128)} async-done(((f32[4,512,512]{2,1,0:T(8,128)}), f32[4,512,512]{2,1,0:T(8,128)}) %all-reduce.3.cloned.1.call-update) | async-done | bytes 4194320 | tf_op jit(solution)/shard_map/psum | solution.py:58
  313.9 3.0 broadcast_multiply_fusion
  316.9 1.6 multiply_reduce_fusion.2
  318.5 4.4 multiply_reduce_fusion.1
  322.9 78.9 %all-reduce = (f32[]{:T(128)}, f32[]{:T(128)}) all-reduce(f32[]{:T(128)} %get-tuple-element.6, f32[]{:T(128)} %get-tuple-element.9), channel_id=1, replica_groups=mesh['dp'=16,'mp'=16] {'dp','mp'}, use_global_device_ids=true, to_apply=%region_2.0 | all-reduce | flops 2 | bytes 16 | tf_op jit(solution)/shard_map/psum | solution.py:75
  403.2 0.7 broadcast_multiply_fusion.1
  403.9 1.6 multiply_reduce_fusion
  405.7 1.0 copy-done.1
  406.8 0.4 fusion.2
  407.2 3.7 fusion.14
  411.0 3.5 fusion.66
  414.5 3.5 fusion.67
  418.0 4.0 fusion.15
  422.0 3.7 fusion.13
  425.8 3.5 fusion.68
  429.3 3.6 fusion.69
  432.9 4.9 %fusion.22 = bf16[1,1,2,512,512]{4,3,2,1,0:T(8,128)(2,1)} fusion(f32[2,512,512]{2,1,0:T(8,128)S(1)} %fusion.13, f32[2,512,512]{2,1,0:T(8,128)S(1)} %fusion.69, f32[512,512]{1,0:T(8,128)S(1)} %fusion.39, pred[2]{0:T(512)(128)(4,1)S(1)} %and_reduce_fusion), kind=kOutput, calls=%fused_computation.24 | convolution fusion | flops 3223322624 | bytes 6291458 | tf_op jit(solution)/shard_map/vmap()/dot_general | solution.py:33
  (23 shorter events, 0.9 us)
Async XLA Ops:
  7.2 76.4 %reduce-scatter.5.cloned.1.call-start = ((), (), s32[]{:S(2)}) async-start(), calls=%async_computation.5 | async-start | bytes 4456448 | tf_op jit(solution)/shard_map/reduce_scatter | solution.py:56
  12.7 1.6 copy-start
  12.7 142.1 %reduce-scatter.3.cloned.1.call-start = ((), (), s32[]{:S(2)}) async-start(), calls=%async_computation.4 | async-start | bytes 4456448 | tf_op jit(solution)/shard_map/reduce_scatter | solution.py:55
  17.6 296.3 %all-reduce.3.cloned.1.call-start = ((), (), s32[]{:S(2)}) async-start(), calls=%async_computation.3 | async-start | bytes 8388608 | tf_op jit(solution)/shard_map/psum | solution.py:58
  20.2 0.7 copy-start.4
  159.6 244.3 %all-to-all-start = ((f32[2,16,32,512]{3,2,0,1:T(8,128)}), f32[2,16,32,512]{3,2,0,1:T(8,128)S(1)}, u32[]{:S(2)}, u32[]{:S(2)}) async-start(f32[2,16,32,512]{3,2,0,1:T(8,128)} %copy.26), calls=%async_computation.2 | async-start | bytes 4194304 | tf_op jit(solution)/shard_map/all_to_all | solution.py:92
  172.5 144.4 %copy-start.2 = (f32[4,32,512]{2,1,0:T(8,128)S(1)}, f32[4,32,512]{2,1,0:T(8,128)}, u32[]{:S(2)}) copy-start(f32[4,32,512]{2,1,0:T(8,128)} %param.9) | copy-start | bytes 786436
  313.9 3.0 copy-start.3
  405.6 1.2 copy-start.1
Sparse Core Ops, SparseCore 0:
  12.9 70.6 reduce-scatter.4
  86.1 68.6 reduce-scatter.2
  157.5 156.3 all-reduce.2
where the time goes:
time: 445 us; the launch traced here: 444 us
  waiting for transfers between devices  274 us (62%)
  blocking collectives  78.9 us (18%)
  matrix products  44.8 us (10%)
  between operations  15.3 us (3%)
  other arithmetic  14.6 us (3%)
  local copies, waits for them, and re-layouts  9.05 us (2%)
  starting transfers between devices  7.43 us (2%)
    psum x1, waiting for transfers between devices, per_device(): grad_whole = lax.psum(local_grads.astype(jnp.float32), 'dp') / data_count  141 us
    psum x1, blocking collectives, per_device(): lax.psum((jnp.sum(adam_step * adam_step), jnp.sum(precond * precond)), ('...  78.9 us
    reduce_scatter x1, waiting for transfers between devices, per_device(): lax.psum_scatter(left_part, 'dp', scatter_dimension=1, tiled=True)  70.3 us
    reduce_scatter x1, waiting for transfers between devices, per_device(): lax.psum_scatter(right_part, 'dp', scatter_dimension=1, tiled=True)  62.5 us
  transfers between devices with their start and end apart: 4, of which 3 were waited for; matrix products, arithmetic and copies ran while one was open for 6% of the time, Pallas kernels for 0%

commit v1 on v0

v1 whole, which is shorter than its diff:
```python
import jax
import jax.numpy as jnp
from jax import lax
from jax.experimental import pallas as pl
from jax.experimental.pallas import tpu as pltpu
from jax.sharding import PartitionSpec as P

MESH = pl.DeviceIdType.MESH
F32 = jnp.float32
BF16 = jnp.bfloat16
BS = 512
T = 128
N_DP = 16
ROWS = BS // N_DP
PIECE = 8 * T
DIAG = 16
OFF_TILES = ((0, 1), (0, 2), (0, 3), (1, 2), (1, 3), (2, 3))
ORDER = (2, 1, 3, 0)

CORE = 0
RAW = 2
STAT = 10
SUMY = 16
DG = 17
GRD = 25
GMX = 28
SCX = 44
AGR = 60
SIB = 64
SC1 = 68
SC2 = 84
AGS = 100
N_SEM = 108
LOC = 8


def dot(a, b):
    return jnp.dot(a, b, preferred_element_type=F32)


def tile_of(t):
    return pl.ds(t * T, T)


def kernel(
    n_mp,
    owners,
    grads,
    roots,
    m1,
    m2,
    update,
    m1n,
    m2n,
    roots_new,
    g_mine,
    g_other,
    left_v,
    right_v,
    tr,
    packed,
    got,
    y_out,
    y_in,
    dg_out,
    dg_in,
    g_send,
    g_recv,
    gm_loc,
    sc_loc,
    gm_rows,
    sc_rows,
    pieces,
    mat,
    mat_b,
    yy,
    yy_b,
    ee,
    ee_b,
    precond,
    s1_out,
    s1_in,
    s2_out,
    s2_in,
    ss,
    rs,
    ls,
):
    me = lax.axis_index("dp")
    col = lax.axis_index("mp")
    x, y, c = me // 4, (me // 2) % 2, me % 2
    even = (x % 2) == c
    keep = x // 2
    blk = 2 * c + y

    def dev(xx, yv, cc):
        return (xx * 4 + yv * 2 + cc, col)

    def xo(k):
        return lax.rem(x + k, 4)

    def rc(src, dst, i_send, i_recv, where):
        return pltpu.make_async_remote_copy(
            src_ref=src,
            dst_ref=dst,
            send_sem=ss.at[i_send],
            recv_sem=rs.at[i_recv],
            device_id=where,
            device_id_type=MESH,
        )

    barrier = pltpu.get_barrier_semaphore()
    for k in range(1, N_DP):
        pl.semaphore_signal(
            barrier, inc=1, device_id=(lax.rem(me + k, N_DP), col), device_id_type=MESH
        )
    for k in range(1, n_mp):
        pl.semaphore_signal(
            barrier, inc=1, device_id=(me, lax.rem(col + k, n_mp)), device_id_type=MESH
        )

    loads = [
        pltpu.make_async_copy(grads.at[0, 2 * c + 1 - y], g_other.at[0], ls.at[0]),
        pltpu.make_async_copy(grads.at[0, 2 * c + y], g_mine.at[0], ls.at[1]),
        pltpu.make_async_copy(roots.at[blk, 0], left_v, ls.at[2]),
    ] + [
        pltpu.make_async_copy(roots.at[b, 1], right_v.at[b], ls.at[3 + b]) for b in range(4)
    ]
    for cp in loads:
        cp.start()
    pl.semaphore_wait(barrier, N_DP - 1 + n_mp - 1)

    sib = dev(x, y, 1 - c)
    sends = []
    core_cp = [
        rc(grads.at[0, 2 * (1 - c) + 1 - y], g_other.at[1], CORE, CORE, sib),
        rc(grads.at[0, 2 * (1 - c) + y], g_mine.at[1], CORE + 1, CORE + 1, sib),
    ]
    for cp in core_cp:
        cp.start()
    raw_cp = []
    for n, k in enumerate(ORDER):
        cols = pl.ds(pl.multiple_of(xo(k) * T, T), T)
        for h in range(2):
            cc = c if h == 0 else 1 - c
            cp = rc(
                grads.at[0, 2 * cc + 1 - y, :, cols],
                g_mine.at[2 + h, :, cols],
                RAW + 2 * n + h,
                RAW + 2 * n + h,
                dev(x, 1 - y, cc),
            )
            cp.start()
            raw_cp.append(cp)
    sends += core_cp + raw_cp

    rows_i = lax.broadcasted_iota(jnp.int32, (T, T), 0)
    cols_i = lax.broadcasted_iota(jnp.int32, (T, T), 1)
    above = rows_i < cols_i
    below = rows_i > cols_i
    on = rows_i == cols_i

    def diag_of(t):
        return jnp.sum(jnp.where(on, t, 0.0), axis=0, keepdims=True)

    def stats(which, g):
        def pack(s, top, bot):
            for n, (i, j) in enumerate(OFF_TILES):
                if i < 2:
                    t = top[i * T : (i + 1) * T, j * T : (j + 1) * T]
                else:
                    t = bot[(i - 2) * T : (i - 1) * T, (j - 2) * T : (j - 1) * T]
                packed[which, s, tile_of(n), :] = t.astype(BF16)
            d = [
                top[0:T, 0:T],
                top[T : 2 * T, T : 2 * T],
                bot[0:T, 0:T],
                bot[T : 2 * T, T : 2 * T],
            ]
            packed[which, s, tile_of(6), :] = jnp.where(above, d[0], d[1]).astype(BF16)
            packed[which, s, tile_of(7), :] = jnp.where(above, d[2], d[3]).astype(BF16)
            dg_out[which, s] = jnp.zeros((8, T), F32)
            for n in range(4):
                dg_out[which, s, n : n + 1, :] = diag_of(d[n])

        for h in range(2):
            tr[h] = g[h].T
        h2 = BS // 2
        top = dot(g[0, :h2, :], tr[0]) + dot(g[1, :h2, :], tr[1])
        bot = dot(g[0, h2:, :], tr[0, :, h2:]) + dot(g[1, h2:, :], tr[1, :, h2:])
        pack(0, top, bot)
        top = dot(tr[0, :h2, :], g[0]) + dot(tr[1, :h2, :], g[1])
        bot = dot(tr[0, h2:, :], g[0, :, h2:]) + dot(tr[1, h2:, :], g[1, :, h2:])
        pack(1, top, bot)

    def stat_cp(which, s):
        xt = 2 * s + c
        k = lax.rem(xt - x + 4, 4)
        slot = jnp.maximum(k - 1, 0)
        return k, rc(
            packed.at[which, s],
            got.at[which, slot],
            STAT + 2 * which + s,
            STAT + 3 * which + slot,
            dev(xt, y, c),
        )

    def dg_cp(which, s):
        yt = 1 - y if which == 0 else y
        return rc(
            dg_out.at[which, s],
            dg_in.at[2 * x + y],
            DG + 2 * which + s,
            DG + 2 * x + y,
            dev(2 * s + c, yt, c),
        )

    def stat_sends(which, act):
        for s in range(2):
            k, cp = stat_cp(which, s)
            pl.when(k != 0)(lambda cp=cp: act(cp))
            cp2 = dg_cp(which, s)
            if which == 0:
                act(cp2)
            else:
                pl.when(k != 0)(lambda cp2=cp2: act(cp2))

    loads[0].wait()
    core_cp[0].wait_recv()
    stats(0, g_other)
    stat_sends(0, lambda cp: cp.start())
    loads[1].wait()
    core_cp[1].wait_recv()
    stats(1, g_mine)
    stat_sends(1, lambda cp: cp.start())

    def raw_sum(n):
        cols = pl.ds(pl.multiple_of(xo(ORDER[n]) * T, T), T)
        raw_cp[2 * n].wait_recv()
        raw_cp[2 * n + 1].wait_recv()
        t = g_mine[0, :, cols].astype(F32) + g_mine[1, :, cols].astype(F32)
        return t + (g_mine[2, :, cols].astype(F32) + g_mine[3, :, cols].astype(F32))

    grd_cp = []

    def grad_chunk(n):
        k = ORDER[n]
        g_send[k - 1] = raw_sum(n)
        cp = rc(g_send.at[k - 1], g_recv.at[k - 1], GRD + k - 1, GRD + k - 1, dev(xo(k), y, c))
        cp.start()
        grd_cp.append(cp)

    def wait_stats(which):
        for slot in range(3):
            rc(
                packed.at[which, 0],
                got.at[which, slot],
                STAT,
                STAT + 3 * which + slot,
                dev(x, 1 - y, c),
            ).wait_recv()

    def stat_tile(which, n):
        t = packed[which, keep, tile_of(n), :].astype(F32)
        for slot in range(3):
            t = t + got[which, slot, tile_of(n), :].astype(F32)
        return t

    y_cp = rc(y_out, y_in, SUMY, SUMY, dev(x, 1 - y, c))

    grad_chunk(0)

    @pl.when(even)
    def _():
        wait_stats(0)
        for n in range(8):
            y_out[tile_of(n), :] = stat_tile(0, n).astype(BF16)
        y_cp.start()

    grad_chunk(1)

    my_piece = 4 * c + 2 * y + keep

    def ring_cp(row, k):
        yr = y if row == 0 else 1 - y
        ref = pieces.at[4 * c + 2 * yr + keep]
        return rc(ref, ref, AGS + 4 * row + k - 1, AGR + 2 * row + keep, dev(xo(k), y, c))

    def ycopy():
        ref = pieces.at[my_piece]
        return rc(ref, ref, AGS + 3, AGR + 2 + keep, dev(x, 1 - y, c))

    @pl.when(even)
    def _():
        wait_stats(1)
        y_cp.wait_recv()
        dsum = dg_out[1, keep]
        for sender in range(8):

            @pl.when(sender != 2 * x + y)
            def _():
                rc(
                    dg_out.at[0, 0], dg_in.at[sender], DG, DG + sender, dev(x, 1 - y, c)
                ).wait_recv()

        for sender in range(8):
            dsum = dsum + jnp.where(sender != 2 * x + y, dg_in[sender], 0.0)
        dsum = dsum * (1.0 / N_DP) + 0.0001

        def full_tile(n):
            return (stat_tile(1, n) + y_in[tile_of(n), :].astype(F32)) * (1.0 / N_DP)

        off_sq = jnp.zeros((T, T), F32)
        for n, (i, j) in enumerate(OFF_TILES):
            t = full_tile(n)
            off_sq = off_sq + t * t
            mat[tile_of(i), tile_of(j)] = t
            mat[tile_of(j), tile_of(i)] = t.T
        for n, (i, j) in ((6, (0, 1)), (7, (2, 3))):
            t = full_tile(n)
            tt = t.T
            d0, d1 = dsum[i : i + 1, :], dsum[j : j + 1, :]
            off_sq = off_sq + jnp.where(on, 0.0, t * t)
            mat[tile_of(i), tile_of(i)] = jnp.where(above, t, jnp.where(below, tt, d0))
            mat[tile_of(j), tile_of(j)] = jnp.where(below, t, jnp.where(above, tt, d1))
        total = 2.0 * jnp.sum(off_sq) + jnp.sum(
            jnp.where(lax.broadcasted_iota(jnp.int32, (8, T), 0) < 4, dsum * dsum, 0.0)
        )
        inv = 1.0 / jnp.sqrt(jnp.full((1, 1), total, F32))
        mat[...] = mat[...] * inv
        mat_b[...] = mat[...].astype(BF16)
        yy[...] = mat[...] * -0.25
        yy_b[...] = yy[...].astype(BF16)
        scale = 1.25
        for _step in range(2):
            ee[...] = (dot(mat_b[...], mat_b[...]) - 10.0 * mat[...]) * (1.0 / 16.0)
            ee_b[...] = ee[...].astype(BF16)
            ee_b[...] = (3.125 * ee[...] + dot(ee_b[...], ee_b[...])).astype(BF16)
            mat[...] = (625.0 / 256.0) * mat[...] + dot(mat_b[...], ee_b[...])
            mat_b[...] = mat[...].astype(BF16)
            yy[...] = (
                1.25 * yy[...] - (scale / 4.0) * mat[...] - 0.25 * dot(yy_b[...], mat_b[...])
            )
            yy_b[...] = yy[...].astype(BF16)
            scale = scale * 1.25
        for n, (i, j) in enumerate(OFF_TILES):
            pieces[my_piece, tile_of(n), :] = yy[tile_of(i), tile_of(j)].astype(BF16)
        for n, (i, j) in ((6, (0, 1)), (7, (2, 3))):
            pieces[my_piece, tile_of(n), :] = jnp.where(
                above, yy[tile_of(i), tile_of(i)], yy[tile_of(j), tile_of(j)]
            ).astype(BF16)
        ds = [diag_of(yy[tile_of(i), tile_of(i)]) + scale for i in range(4)]
        pieces[my_piece, PIECE : PIECE + DIAG, :] = jnp.concatenate(
            ds + [jnp.zeros((DIAG - 4, T), F32)], axis=0
        ).astype(BF16)
        ycopy().start()
        for k in (1, 3, 2):
            ring_cp(0, k).start()

    grad_chunk(2)

    def piece_at(row, s):
        yr = y if row == 0 else 1 - y
        return pieces.at[4 * c + 2 * yr + s]

    def other_piece_at(row, s):
        yr = y if row == 0 else 1 - y
        return pieces.at[4 * (1 - c) + 2 * yr + s]

    def sib_cp(row, s):
        return rc(piece_at(row, s), piece_at(row, s), SIB + 2 * row + s, SIB + 2 * row + s, sib)

    def ag_wait(row, s):
        ref = piece_at(row, s)
        rc(ref, ref, AGR, AGR + 2 * row + s, dev(x, 1 - y, c)).wait_recv()

    own = raw_sum(3)
    for k in (2, 1, 3):
        grd_cp[(2, 1, 3).index(k)].wait_recv()
        own = own + g_recv[k - 1]
    gm_loc[...] = own * (1.0 / N_DP)
    my_cols = pl.ds(pl.multiple_of(x * T, T), T)

    def gm_cp(k):
        to = lax.rem(me + k, N_DP)
        r = pl.ds(pl.multiple_of(to * ROWS, ROWS), ROWS)
        return rc(gm_loc.at[r], gm_rows.at[blk, :, my_cols], GMX + k, GMX + k, (to, col))

    def sc_cp(k):
        to = lax.rem(me + k, N_DP)
        r = pl.ds(pl.multiple_of(to * ROWS, ROWS), ROWS)
        return rc(sc_loc.at[r], sc_rows.at[blk, :, my_cols], SCX + k, SCX + k, (to, col))

    my_rows = pl.ds(pl.multiple_of(me * ROWS, ROWS), ROWS)
    for k in range(1, N_DP):
        gm_cp(k).start()
    loads[2].wait()
    sc_loc[...] = dot(left_v[...], gm_loc[...].astype(BF16)).astype(BF16)
    for k in range(1, N_DP):
        sc_cp(k).start()
    gm_rows[blk, :, my_cols] = gm_loc[my_rows, :]
    sc_rows[blk, :, my_cols] = sc_loc[my_rows, :]

    @pl.when(even)
    def _():
        sib_cp(0, keep).start()
        ag_wait(1, keep)
        for k in (1, 3, 2):
            ring_cp(1, k).start()
        sib_cp(1, keep).start()
        ag_wait(0, 1 - keep)
        sib_cp(0, 1 - keep).start()

    @pl.when(jnp.logical_not(even))
    def _():
        for s in range(2):
            ag_wait(0, s)
            sib_cp(0, s).start()

    for k in range(1, N_DP):
        gm_cp(k).wait_recv()
    g = gm_rows[...]
    first = 0.9 * m1[...] + 0.1 * g
    second = 0.95 * m2[...] + 0.05 * g * g
    m1n[...] = first
    m2n[...] = second
    adam = first / (jnp.sqrt(second) + 1e-08)
    adam_sq = jnp.sum(adam * adam)
    for b in range(4):
        loads[3 + b].wait()
    for k in range(1, N_DP):
        sc_cp(k).wait_recv()
    pre_sq = jnp.zeros((ROWS, BS), F32)
    for b in range(4):
        p = dot(sc_rows[b], right_v[b])
        precond[b] = p
        pre_sq = pre_sq + p * p
    pre_sq = jnp.sum(pre_sq)
    row8 = lax.broadcasted_iota(jnp.int32, (8, T), 0)
    mine = jnp.where(row8 == 0, adam_sq, jnp.where(row8 == 1, pre_sq, 0.0))
    s1_out[...] = mine

    def s1_cp(k):
        return rc(s1_out, s1_in.at[k], SC1 + k, SC1 + k, (lax.rem(me + k, N_DP), col))

    def s2_cp(k):
        return rc(s2_out, s2_in.at[k], SC2 + k, SC2 + k, (me, lax.rem(col + k, n_mp)))

    for k in range(1, N_DP):
        s1_cp(k).start()
    for k in range(1, N_DP):
        s1_cp(k).wait_recv()
    for k in range(1, N_DP):
        mine = mine + s1_in[k]
    s2_out[...] = mine
    for k in range(1, n_mp):
        s2_cp(k).start()

    @pl.when(even)
    def _():
        ag_wait(1, 1 - keep)
        sib_cp(1, 1 - keep).start()

    @pl.when(jnp.logical_not(even))
    def _():
        for s in range(2):
            ag_wait(1, s)
            sib_cp(1, s).start()

    for k in range(1, n_mp):
        s2_cp(k).wait_recv()
    for k in range(1, n_mp):
        mine = mine + s2_in[k]
    ratio = jnp.sqrt(mine[0:1, :]) / jnp.sqrt(mine[1:2, :] + 1e-06)
    for b in range(4):
        for n in range(4):
            update[b, :, tile_of(n)] = precond[b, :, tile_of(n)] * ratio

    for row in range(2):
        for s in range(2):
            ref = other_piece_at(row, s)
            rc(ref, ref, SIB, SIB + 2 * row + s, sib).wait_recv()

    first_id, second_id, n_mine = jnp.int32(0), jnp.int32(0), jnp.int32(0)
    for i in range(8):
        hit = owners[i, 0] == me
        first_id = jnp.where(hit & (n_mine == 0), i, first_id)
        second_id = jnp.where(hit & (n_mine == 1), i, second_id)
        n_mine = n_mine + jnp.where(hit, 1, 0)
    for slot, idx in ((0, first_id), (1, second_id)):
        filled = n_mine > slot

        def piece_tile(n):
            return jnp.where(filled, pieces[idx, tile_of(n), :].astype(F32), 0.0)

        for n, (i, j) in enumerate(OFF_TILES):
            t = piece_tile(n)
            roots_new[slot, tile_of(i), tile_of(j)] = t.astype(BF16)
            roots_new[slot, tile_of(j), tile_of(i)] = t.T.astype(BF16)
        dg = jnp.where(filled, pieces[idx, PIECE : PIECE + DIAG, :].astype(F32), 0.0)
        for n, (i, j) in ((6, (0, 1)), (7, (2, 3))):
            t = piece_tile(n)
            tt = t.T
            d0, d1 = dg[i : i + 1, :], dg[j : j + 1, :]
            roots_new[slot, tile_of(i), tile_of(i)] = jnp.where(
                above, t, jnp.where(below, tt, d0)
            ).astype(BF16)
            roots_new[slot, tile_of(j), tile_of(j)] = jnp.where(
                below, t, jnp.where(above, tt, d1)
            ).astype(BF16)

    for cp in sends + grd_cp:
        cp.wait_send()
    stat_sends(0, lambda cp: cp.wait_send())
    stat_sends(1, lambda cp: cp.wait_send())

    @pl.when(even)
    def _():
        y_cp.wait_send()
        ycopy().wait_send()
        for row in range(2):
            for k in (1, 3, 2):
                ring_cp(row, k).wait_send()

    for row in range(2):
        for s in range(2):
            sib_cp(row, s).wait_send()
    for k in range(1, N_DP):
        gm_cp(k).wait_send()
        sc_cp(k).wait_send()
        s1_cp(k).wait_send()
    for k in range(1, n_mp):
        s2_cp(k).wait_send()


def per_device(grads, owners, roots_prev, moment_first, moment_second):
    n_mp = lax.axis_size("mp")
    any_spec = pl.BlockSpec(memory_space=pl.ANY)
    vmem = pl.BlockSpec(memory_space=pltpu.VMEM)
    small = jax.ShapeDtypeStruct((4, ROWS, BS), F32)

    def body(*refs):
        kernel(n_mp, *refs)

    update, m1n, m2n, roots_new = pl.pallas_call(
        body,
        out_shape=(small, small, small, jax.ShapeDtypeStruct((2, BS, BS), BF16)),
        in_specs=[pl.BlockSpec(memory_space=pltpu.SMEM), any_spec, any_spec, vmem, vmem],
        out_specs=(vmem, vmem, vmem, vmem),
        scratch_shapes=[
            pltpu.VMEM((4, BS, BS), BF16),
            pltpu.VMEM((2, BS, BS), BF16),
            pltpu.VMEM((BS, BS), BF16),
            pltpu.VMEM((4, BS, BS), BF16),
            pltpu.VMEM((2, BS, BS), BF16),
            pltpu.VMEM((2, 2, PIECE, T), BF16),
            pltpu.VMEM((2, 3, PIECE, T), BF16),
            pltpu.VMEM((PIECE, T), BF16),
            pltpu.VMEM((PIECE, T), BF16),
            pltpu.VMEM((2, 2, 8, T), F32),
            pltpu.VMEM((8, 8, T), F32),
            pltpu.VMEM((3, BS, T), F32),
            pltpu.VMEM((3, BS, T), F32),
            pltpu.VMEM((BS, T), F32),
            pltpu.VMEM((BS, T), BF16),
            pltpu.VMEM((4, ROWS, BS), F32),
            pltpu.VMEM((4, ROWS, BS), BF16),
            pltpu.VMEM((8, PIECE + DIAG, T), BF16),
            pltpu.VMEM((BS, BS), F32),
            pltpu.VMEM((BS, BS), BF16),
            pltpu.VMEM((BS, BS), F32),
            pltpu.VMEM((BS, BS), BF16),
            pltpu.VMEM((BS, BS), F32),
            pltpu.VMEM((BS, BS), BF16),
            pltpu.VMEM((4, ROWS, BS), F32),
            pltpu.VMEM((8, T), F32),
            pltpu.VMEM((N_DP, 8, T), F32),
            pltpu.VMEM((8, T), F32),
            pltpu.VMEM((max(n_mp, 2), 8, T), F32),
            pltpu.SemaphoreType.DMA((N_SEM,)),
            pltpu.SemaphoreType.DMA((N_SEM,)),
            pltpu.SemaphoreType.DMA((LOC,)),
        ],
        compiler_params=pltpu.CompilerParams(
            collective_id=0, has_side_effects=True, vmem_limit_bytes=48 * 2**20
        ),
        name="shampoo",
    )(owners, grads, roots_prev, moment_first, moment_second)
    return update, m1n, m2n, roots_new[None, None]


def solution(mesh):
    return jax.shard_map(
        per_device,
        mesh=mesh,
        in_specs=(
            P("dp", "mp", None, None),
            P("mp", None),
            P("mp", None, None, None),
            P("mp", "dp", None),
            P("mp", "dp", None),
        ),
        out_specs=(
            P("mp", "dp", None),
            P("mp", "dp", None),
            P("mp", "dp", None),
            P("dp", "mp", None, None, None),
        ),
        check_vma=False,
    )
```

time: 445 us -> 82 us (0.18)
  waiting for transfers between devices: 274 us -> 0 us
  blocking collectives: 78.9 us -> 0 us
  Pallas kernels: 0 us -> 73.9 us
  matrix products: 44.8 us -> 0 us
  between operations: 15.3 us -> 0.64 us
  other arithmetic: 14.6 us -> 0 us
  starting transfers between devices: 7.43 us -> 0 us
    psum x1 -> x0, waiting for transfers between devices: 141 us -> none  [per_device(): grad_whole = lax.psum(local_grads.astype(jnp.float32), 'dp') / data_count]
    reduce_scatter x2 -> x0, waiting for transfers between devices: 133 us -> none  [the longest x1 70.3 us: per_device(): lax.psum_scatter(left_part, 'dp', scatter_dimension=1, tiled=True)]
    psum x1 -> x0, blocking collectives: 78.9 us -> none  [per_device(): lax.psum((jnp.sum(adam_step * adam_step), jnp.sum(precond * precond)), ('...]
    pallas_call x0 -> x1, Pallas kernels: none -> 73.9 us  [per_device(): pl.pallas_call(body, out_shape=(small, small, small, jax.ShapeDtypeStruct...]
    dot_general x12 -> x0, matrix products: 44.8 us -> none  [the longest x2 8.69 us: inverse_root(): iterate = jnp.dot(iterate, factor, precision=HIGHEST_PRECISION)]
    all_to_all x1 -> x0, starting transfers between devices: 7.31 us -> none  [per_device(): lax.all_to_all(outgoing, 'dp', split_axis=1, concat_axis=1, tiled=True)]
  transfers between devices with their start and end apart: 4 -> 0, of which waited for: 3 -> 0; matrix products, arithmetic and copies ran while one was open for 6% -> 0% of each run, Pallas kernels for 0% -> 0%
where the time goes in v1:
time: 82 us; the launch traced here: 81.9 us
  Pallas kernels  73.9 us (90%)
  local copies, waits for them, and re-layouts  7.3 us (9%)
    pallas_call x1, Pallas kernels, per_device(): pl.pallas_call(body, out_shape=(small, small, small, jax.ShapeDtypeStruct...  73.9 us
    unnamed x11, local copies, waits for them, and re-layouts  7.3 us

profile of v1, /device:TPU:1, one launch (start us, length us, event | category | flops | bytes accessed | tf_op | source)
XLA Modules:
  0.0 81.9 jit_solution(12101048848820170701)
XLA Ops:
  0.6 0.7 copy.9.refs_0_
  1.4 0.0 copy-start
  1.4 1.6 %copy-done = bf16[1,4,512,512]{3,2,1,0:T(8,128)(2,1)S(1)} copy-done((bf16[1,4,512,512]{3,2,1,0:T(8,128)(2,1)S(1)}, bf16[1,4,512,512]{3,2,1,0:T(8,128)(2,1)}, u32[]{:S(2)}) %copy-start) | copy-done | bytes 2097176
  3.0 0.0 copy-start.1
  3.0 0.9 %copy-done.1 = f32[4,32,512]{2,1,0:T(8,128)S(1)} copy-done((f32[4,32,512]{2,1,0:T(8,128)S(1)}, f32[4,32,512]{2,1,0:T(8,128)}, u32[]{:S(2)}) %copy-start.1) | copy-done | bytes 262168
  3.9 0.0 copy-start.2
  3.9 0.9 %copy-done.2 = f32[4,32,512]{2,1,0:T(8,128)S(1)} copy-done((f32[4,32,512]{2,1,0:T(8,128)S(1)}, f32[4,32,512]{2,1,0:T(8,128)}, u32[]{:S(2)}) %copy-start.2) | copy-done | bytes 262168
  4.9 73.9 %shampoo.1 = (f32[4,32,512]{2,1,0:T(8,128)S(1)}, f32[4,32,512]{2,1,0:T(8,128)S(1)}, f32[4,32,512]{2,1,0:T(8,128)S(1)}, bf16[2,512,512]{2,1,0:T(8,128)(2,1)S(1)}) custom-call(s32[8,1]{1,0:T(8,128)S(1)} %copy.9.refs_0_, bf16[1,4,512,512]{3,2,1,0:T(8,128)(2,1)S(1)} %copy-done, bf16[4,2,512,512]{3,2,1,0:T(8,128)(2,1)} %refs_2_.1, f32[4,32,512]{2,1,0:T(8,128)S(1)} %copy-done.1, ...), custom_call_target="tpu_custom_call" | custom-call | tf_op jit(solution)/shard_map/shampoo/pallas_call | solution.py:545
  78.8 0.7 copy.14
  79.5 0.7 copy.15
  80.2 0.7 copy.16
  80.9 1.0 %copy.17 = bf16[1,1,2,512,512]{4,3,2,1,0:T(8,128)(2,1)} copy(bf16[1,1,2,512,512]{4,3,2,1,0:T(8,128)(2,1)S(1)} %bitcast.1) | data formatting | bytes 2097152
Async XLA Ops:
  1.4 1.6 %copy-start = (bf16[1,4,512,512]{3,2,1,0:T(8,128)(2,1)S(1)}, bf16[1,4,512,512]{3,2,1,0:T(8,128)(2,1)}, u32[]{:S(2)}) copy-start(bf16[1,4,512,512]{3,2,1,0:T(8,128)(2,1)} %refs_1_.1) | copy-start | bytes 6291460
  3.0 0.9 %copy-start.1 = (f32[4,32,512]{2,1,0:T(8,128)S(1)}, f32[4,32,512]{2,1,0:T(8,128)}, u32[]{:S(2)}) copy-start(f32[4,32,512]{2,1,0:T(8,128)} %refs_3_.1) | copy-start | bytes 786436
  3.9 0.9 %copy-start.2 = (f32[4,32,512]{2,1,0:T(8,128)S(1)}, f32[4,32,512]{2,1,0:T(8,128)}, u32[]{:S(2)}) copy-start(f32[4,32,512]{2,1,0:T(8,128)} %refs_4_.1) | copy-start | bytes 786436

commit v2 on v1

--- a/solution.py
+++ b/solution.py
@@ -31,7 +31,7 @@
 SC2 = 84
 AGS = 100
 N_SEM = 108
-LOC = 8
+LOC = 9
 
 
 def dot(a, b):
@@ -47,8 +47,8 @@
     owners,
     grads,
     roots,
-    m1,
-    m2,
+    m1_hbm,
+    m2_hbm,
     update,
     m1n,
     m2n,
@@ -82,6 +82,8 @@
     s1_in,
     s2_out,
     s2_in,
+    m1,
+    m2,
     ss,
     rs,
     ls,
@@ -125,6 +127,9 @@
         pltpu.make_async_copy(roots.at[blk, 0], left_v, ls.at[2]),
     ] + [
         pltpu.make_async_copy(roots.at[b, 1], right_v.at[b], ls.at[3 + b]) for b in range(4)
+    ] + [
+        pltpu.make_async_copy(m1_hbm, m1, ls.at[7]),
+        pltpu.make_async_copy(m2_hbm, m2, ls.at[8]),
     ]
     for cp in loads:
         cp.start()
@@ -290,10 +295,54 @@
         ref = pieces.at[my_piece]
         return rc(ref, ref, AGS + 3, AGR + 2 + keep, dev(x, 1 - y, c))
 
+    grad_chunk(2)
+
+    def piece_at(row, s):
+        yr = y if row == 0 else 1 - y
+        return pieces.at[4 * c + 2 * yr + s]
+
+    def other_piece_at(row, s):
+        yr = y if row == 0 else 1 - y
+        return pieces.at[4 * (1 - c) + 2 * yr + s]
+
+    def sib_cp(row, s):
+        return rc(piece_at(row, s), piece_at(row, s), SIB + 2 * row + s, SIB + 2 * row + s, sib)
+
+    def ag_wait(row, s):
+        ref = piece_at(row, s)
+        rc(ref, ref, AGR, AGR + 2 * row + s, dev(x, 1 - y, c)).wait_recv()
+
+    own = raw_sum(3)
+    for k in (2, 1, 3):
+        grd_cp[(2, 1, 3).index(k)].wait_recv()
+        own = own + g_recv[k - 1]
+    gm_loc[...] = own * (1.0 / N_DP)
+    my_cols = pl.ds(pl.multiple_of(x * T, T), T)
+
+    def gm_cp(k):
+        to = lax.rem(me + k, N_DP)
+        r = pl.ds(pl.multiple_of(to * ROWS, ROWS), ROWS)
+        return rc(gm_loc.at[r], gm_rows.at[blk, :, my_cols], GMX + k, GMX + k, (to, col))
+
+    def sc_cp(k):
+        to = lax.rem(me + k, N_DP)
+        r = pl.ds(pl.multiple_of(to * ROWS, ROWS), ROWS)
+        return rc(sc_loc.at[r], sc_rows.at[blk, :, my_cols], SCX + k, SCX + k, (to, col))
+
+    my_rows = pl.ds(pl.multiple_of(me * ROWS, ROWS), ROWS)
+    for k in range(1, N_DP):
+        gm_cp(k).start()
+    loads[2].wait()
+    sc_loc[...] = dot(left_v[...], gm_loc[...].astype(BF16)).astype(BF16)
+    for k in range(1, N_DP):
+        sc_cp(k).start()
+    gm_rows[blk, :, my_cols] = gm_loc[my_rows, :]
+    sc_rows[blk, :, my_cols] = sc_loc[my_rows, :]
+
     @pl.when(even)
     def _():
+        y_cp.wait_recv()
         wait_stats(1)
-        y_cp.wait_recv()
         dsum = dg_out[1, keep]
         for sender in range(8):
 
@@ -357,68 +406,10 @@
         for k in (1, 3, 2):
             ring_cp(0, k).start()
 
-    grad_chunk(2)
-
-    def piece_at(row, s):
-        yr = y if row == 0 else 1 - y
-        return pieces.at[4 * c + 2 * yr + s]
-
-    def other_piece_at(row, s):
-        yr = y if row == 0 else 1 - y
-        return pieces.at[4 * (1 - c) + 2 * yr + s]
-
-    def sib_cp(row, s):
-        return rc(piece_at(row, s), piece_at(row, s), SIB + 2 * row + s, SIB + 2 * row + s, sib)
-
-    def ag_wait(row, s):
-        ref = piece_at(row, s)
-        rc(ref, ref, AGR, AGR + 2 * row + s, dev(x, 1 - y, c)).wait_recv()
-
-    own = raw_sum(3)
-    for k in (2, 1, 3):
-        grd_cp[(2, 1, 3).index(k)].wait_recv()
-        own = own + g_recv[k - 1]
-    gm_loc[...] = own * (1.0 / N_DP)
-    my_cols = pl.ds(pl.multiple_of(x * T, T), T)
-
-    def gm_cp(k):
-        to = lax.rem(me + k, N_DP)
-        r = pl.ds(pl.multiple_of(to * ROWS, ROWS), ROWS)
-        return rc(gm_loc.at[r], gm_rows.at[blk, :, my_cols], GMX + k, GMX + k, (to, col))
-
-    def sc_cp(k):
-        to = lax.rem(me + k, N_DP)
-        r = pl.ds(pl.multiple_of(to * ROWS, ROWS), ROWS)
-        return rc(sc_loc.at[r], sc_rows.at[blk, :, my_cols], SCX + k, SCX + k, (to, col))
-
-    my_rows = pl.ds(pl.multiple_of(me * ROWS, ROWS), ROWS)
-    for k in range(1, N_DP):
-        gm_cp(k).start()
-    loads[2].wait()
-    sc_loc[...] = dot(left_v[...], gm_loc[...].astype(BF16)).astype(BF16)
-    for k in range(1, N_DP):
-        sc_cp(k).start()
-    gm_rows[blk, :, my_cols] = gm_loc[my_rows, :]
-    sc_rows[blk, :, my_cols] = sc_loc[my_rows, :]
-
-    @pl.when(even)
-    def _():
-        sib_cp(0, keep).start()
-        ag_wait(1, keep)
-        for k in (1, 3, 2):
-            ring_cp(1, k).start()
-        sib_cp(1, keep).start()
-        ag_wait(0, 1 - keep)
-        sib_cp(0, 1 - keep).start()
-
-    @pl.when(jnp.logical_not(even))
-    def _():
-        for s in range(2):
-            ag_wait(0, s)
-            sib_cp(0, s).start()
-
     for k in range(1, N_DP):
         gm_cp(k).wait_recv()
+    loads[7].wait()
+    loads[8].wait()
     g = gm_rows[...]
     first = 0.9 * m1[...] + 0.1 * g
     second = 0.95 * m2[...] + 0.05 * g * g
@@ -448,6 +439,21 @@
 
     for k in range(1, N_DP):
         s1_cp(k).start()
+
+    @pl.when(even)
+    def _():
+        sib_cp(0, keep).start()
+        ag_wait(1, keep)
+        for k in (1, 3, 2):
+            ring_cp(1, k).start()
+        sib_cp(1, keep).start()
+
+    @pl.when(jnp.logical_not(even))
+    def _():
+        for s in range(2):
+            ag_wait(0, s)
+            sib_cp(0, s).start()
+
     for k in range(1, N_DP):
         s1_cp(k).wait_recv()
     for k in range(1, N_DP):
@@ -458,23 +464,15 @@
 
     @pl.when(even)
     def _():
-        ag_wait(1, 1 - keep)
-        sib_cp(1, 1 - keep).start()
+        for row in range(2):
+            ag_wait(row, 1 - keep)
+            sib_cp(row, 1 - keep).start()
 
     @pl.when(jnp.logical_not(even))
     def _():
         for s in range(2):
             ag_wait(1, s)
             sib_cp(1, s).start()
-
-    for k in range(1, n_mp):
-        s2_cp(k).wait_recv()
-    for k in range(1, n_mp):
-        mine = mine + s2_in[k]
-    ratio = jnp.sqrt(mine[0:1, :]) / jnp.sqrt(mine[1:2, :] + 1e-06)
-    for b in range(4):
-        for n in range(4):
-            update[b, :, tile_of(n)] = precond[b, :, tile_of(n)] * ratio
 
     for row in range(2):
         for s in range(2):
@@ -509,6 +507,15 @@
                 below, t, jnp.where(above, tt, d1)
             ).astype(BF16)
 
+    for k in range(1, n_mp):
+        s2_cp(k).wait_recv()
+    for k in range(1, n_mp):
+        mine = mine + s2_in[k]
+    ratio = jnp.sqrt(mine[0:1, :]) / jnp.sqrt(mine[1:2, :] + 1e-06)
+    for b in range(4):
+        for n in range(4):
+            update[b, :, tile_of(n)] = precond[b, :, tile_of(n)] * ratio
+
     for cp in sends + grd_cp:
         cp.wait_send()
     stat_sends(0, lambda cp: cp.wait_send())
@@ -533,8 +540,22 @@
         s2_cp(k).wait_send()
 
 
+def store(u, a, b, r, u_out, a_out, b_out, r_out, sems):
+    copies = [
+        pltpu.make_async_copy(r, r_out.at[0, 0], sems.at[0]),
+        pltpu.make_async_copy(u, u_out, sems.at[1]),
+        pltpu.make_async_copy(a, a_out, sems.at[2]),
+        pltpu.make_async_copy(b, b_out, sems.at[3]),
+    ]
+    for cp in copies:
+        cp.start()
+    for cp in copies:
+        cp.wait()
+
+
 def per_device(grads, owners, roots_prev, moment_first, moment_second):
     n_mp = lax.axis_size("mp")
+    hbm = pl.BlockSpec(memory_space=pltpu.HBM)
     any_spec = pl.BlockSpec(memory_space=pl.ANY)
     vmem = pl.BlockSpec(memory_space=pltpu.VMEM)
     small = jax.ShapeDtypeStruct((4, ROWS, BS), F32)
@@ -545,7 +566,7 @@
     update, m1n, m2n, roots_new = pl.pallas_call(
         body,
         out_shape=(small, small, small, jax.ShapeDtypeStruct((2, BS, BS), BF16)),
-        in_specs=[pl.BlockSpec(memory_space=pltpu.SMEM), any_spec, any_spec, vmem, vmem],
+        in_specs=[pl.BlockSpec(memory_space=pltpu.SMEM), hbm, hbm, hbm, hbm],
         out_specs=(vmem, vmem, vmem, vmem),
         scratch_shapes=[
             pltpu.VMEM((4, BS, BS), BF16),
@@ -577,16 +598,25 @@
             pltpu.VMEM((N_DP, 8, T), F32),
             pltpu.VMEM((8, T), F32),
             pltpu.VMEM((max(n_mp, 2), 8, T), F32),
+            pltpu.VMEM((4, ROWS, BS), F32),
+            pltpu.VMEM((4, ROWS, BS), F32),
             pltpu.SemaphoreType.DMA((N_SEM,)),
             pltpu.SemaphoreType.DMA((N_SEM,)),
             pltpu.SemaphoreType.DMA((LOC,)),
         ],
         compiler_params=pltpu.CompilerParams(
-            collective_id=0, has_side_effects=True, vmem_limit_bytes=48 * 2**20
+            collective_id=0, has_side_effects=True, vmem_limit_bytes=62 * 2**20
         ),
         name="shampoo",
     )(owners, grads, roots_prev, moment_first, moment_second)
-    return update, m1n, m2n, roots_new[None, None]
+    return pl.pallas_call(
+        store,
+        out_shape=(small, small, small, jax.ShapeDtypeStruct((1, 1, 2, BS, BS), BF16)),
+        in_specs=[vmem] * 4,
+        out_specs=[hbm] * 4,
+        scratch_shapes=[pltpu.SemaphoreType.DMA((4,))],
+        name="store",
+    )(update, m1n, m2n, roots_new)
 
 
 def solution(mesh):

time: 82 us -> 69.8 us (0.85)
  Pallas kernels: 73.9 us -> 67.7 us
  local copies, waits for them, and re-layouts: 7.3 us -> 1.32 us
    pallas_call x1, Pallas kernels: 73.9 us -> 65 us  [per_device(): pl.pallas_call(body, out_shape=(small, small, small, jax.ShapeDtypeStruct...]
    unnamed x11 -> x1, local copies, waits for them, and re-layouts: 7.3 us -> 1.32 us
    pallas_call x0 -> x1, Pallas kernels: none -> 2.73 us  [per_device(): pl.pallas_call(store, out_shape=(small, small, small, jax.ShapeDtypeStruc...]
where the time goes in v2:
time: 69.8 us; the launch traced here: 69.6 us
  Pallas kernels  67.7 us (97%)
  local copies, waits for them, and re-layouts  1.32 us (2%)
    pallas_call x1, Pallas kernels, per_device(): pl.pallas_call(body, out_shape=(small, small, small, jax.ShapeDtypeStruct...  65 us
    pallas_call x1, Pallas kernels, per_device(): pl.pallas_call(store, out_shape=(small, small, small, jax.ShapeDtypeStruc...  2.73 us

profile of v2, /device:TPU:1, one launch (start us, length us, event | category | flops | bytes accessed | tf_op | source)
XLA Modules:
  0.0 69.6 jit_solution(15190757344398912424)
XLA Ops:
  0.6 1.3 %copy.9.refs_0_ = s32[8,1]{1,0:T(8,128)} copy(s32[8,1]{0,1:T(1,128)} %param.6) | data formatting | bytes 64 | tf_op args[1]
  2.0 65.0 %shampoo.1 = (f32[4,32,512]{2,1,0:T(8,128)}, f32[4,32,512]{2,1,0:T(8,128)}, f32[4,32,512]{2,1,0:T(8,128)}, bf16[2,512,512]{2,1,0:T(8,128)(2,1)}) custom-call(s32[8,1]{1,0:T(8,128)} %copy.9.refs_0_, bf16[1,4,512,512]{3,2,1,0:T(8,128)(2,1)} %refs_1_.1, bf16[4,2,512,512]{3,2,1,0:T(8,128)(2,1)} %refs_2_.1, f32[4,32,512]{2,1,0:T(8,128)} %refs_3_.1, ...), custom_call_target="tpu_custom_call" | custom-call | tf_op jit(solution)/shard_map/shampoo/pallas_call | solution.py:566
  66.9 2.7 %store.1 = (f32[4,32,512]{2,1,0:T(8,128)}, f32[4,32,512]{2,1,0:T(8,128)}, f32[4,32,512]{2,1,0:T(8,128)}, bf16[1,1,2,512,512]{4,3,2,1,0:T(8,128)(2,1)}) custom-call(f32[4,32,512]{2,1,0:T(8,128)} %get-tuple-element.8.u, f32[4,32,512]{2,1,0:T(8,128)} %get-tuple-element.9.a, f32[4,32,512]{2,1,0:T(8,128)} %get-tuple-element.10.b, ...), custom_call_target="tpu_custom_call" | custom-call | tf_op jit(solution)/shard_map/store/pallas_call | solution.py:612

commit v3 on v2

--- a/solution.py
+++ b/solution.py
@@ -20,7 +20,6 @@
 CORE = 0
 RAW = 2
 STAT = 10
-SUMY = 16
 DG = 17
 GRD = 25
 GMX = 28
@@ -30,7 +29,8 @@
 SC1 = 68
 SC2 = 84
 AGS = 100
-N_SEM = 108
+YS = 108
+N_SEM = 116
 LOC = 9
 
 
@@ -271,7 +271,10 @@
             t = t + got[which, slot, tile_of(n), :].astype(F32)
         return t
 
-    y_cp = rc(y_out, y_in, SUMY, SUMY, dev(x, 1 - y, c))
+    y_cp = [
+        rc(y_out.at[tile_of(n)], y_in.at[tile_of(n)], YS + n, YS + n, dev(x, 1 - y, c))
+        for n in range(8)
+    ]
 
     grad_chunk(0)
 
@@ -280,7 +283,7 @@
         wait_stats(0)
         for n in range(8):
             y_out[tile_of(n), :] = stat_tile(0, n).astype(BF16)
-        y_cp.start()
+            y_cp[n].start()
 
     grad_chunk(1)
 
@@ -307,6 +310,10 @@
 
     def sib_cp(row, s):
         return rc(piece_at(row, s), piece_at(row, s), SIB + 2 * row + s, SIB + 2 * row + s, sib)
+
+    def over_cp(s):
+        ref = piece_at(0, s)
+        return rc(ref, ref, AGS + s, AGR + 2 + s, dev(x, 1 - y, c))
 
     def ag_wait(row, s):
         ref = piece_at(row, s)
@@ -341,7 +348,8 @@
 
     @pl.when(even)
     def _():
-        y_cp.wait_recv()
+        for cp in y_cp:
+            cp.wait_recv()
         wait_stats(1)
         dsum = dg_out[1, keep]
         for sender in range(8):
@@ -427,8 +435,7 @@
         precond[b] = p
         pre_sq = pre_sq + p * p
     pre_sq = jnp.sum(pre_sq)
-    row8 = lax.broadcasted_iota(jnp.int32, (8, T), 0)
-    mine = jnp.where(row8 == 0, adam_sq, jnp.where(row8 == 1, pre_sq, 0.0))
+    mine = jnp.where(lax.broadcasted_iota(jnp.int32, (1, T), 1) < T // 2, adam_sq, pre_sq)
     s1_out[...] = mine
 
     def s1_cp(k):
@@ -444,14 +451,14 @@
     def _():
         sib_cp(0, keep).start()
         ag_wait(1, keep)
-        for k in (1, 3, 2):
-            ring_cp(1, k).start()
+        ring_cp(1, 2).start()
         sib_cp(1, keep).start()
 
     @pl.when(jnp.logical_not(even))
     def _():
         for s in range(2):
             ag_wait(0, s)
+            over_cp(s).start()
             sib_cp(0, s).start()
 
     for k in range(1, N_DP):
@@ -481,7 +488,7 @@
 
     first_id, second_id, n_mine = jnp.int32(0), jnp.int32(0), jnp.int32(0)
     for i in range(8):
-        hit = owners[i, 0] == me
+        hit = owners[0, i] == me
         first_id = jnp.where(hit & (n_mine == 0), i, first_id)
         second_id = jnp.where(hit & (n_mine == 1), i, second_id)
         n_mine = n_mine + jnp.where(hit, 1, 0)
@@ -511,10 +518,9 @@
         s2_cp(k).wait_recv()
     for k in range(1, n_mp):
         mine = mine + s2_in[k]
-    ratio = jnp.sqrt(mine[0:1, :]) / jnp.sqrt(mine[1:2, :] + 1e-06)
+    ratio = jnp.sqrt(mine[:, :1]) / jnp.sqrt(mine[:, T - 1 :] + 1e-06)
     for b in range(4):
-        for n in range(4):
-            update[b, :, tile_of(n)] = precond[b, :, tile_of(n)] * ratio
+        update[b] = precond[b] * ratio
 
     for cp in sends + grd_cp:
         cp.wait_send()
@@ -523,11 +529,17 @@
 
     @pl.when(even)
     def _():
-        y_cp.wait_send()
+        for cp in y_cp:
+            cp.wait_send()
         ycopy().wait_send()
-        for row in range(2):
-            for k in (1, 3, 2):
-                ring_cp(row, k).wait_send()
+        for k in (1, 3, 2):
+            ring_cp(0, k).wait_send()
+        ring_cp(1, 2).wait_send()
+
+    @pl.when(jnp.logical_not(even))
+    def _():
+        for s in range(2):
+            over_cp(s).wait_send()
 
     for row in range(2):
         for s in range(2):
@@ -594,10 +606,10 @@
             pltpu.VMEM((BS, BS), F32),
             pltpu.VMEM((BS, BS), BF16),
             pltpu.VMEM((4, ROWS, BS), F32),
-            pltpu.VMEM((8, T), F32),
-            pltpu.VMEM((N_DP, 8, T), F32),
-            pltpu.VMEM((8, T), F32),
-            pltpu.VMEM((max(n_mp, 2), 8, T), F32),
+            pltpu.VMEM((1, T), F32),
+            pltpu.VMEM((N_DP, 1, T), F32),
+            pltpu.VMEM((1, T), F32),
+            pltpu.VMEM((max(n_mp, 2), 1, T), F32),
             pltpu.VMEM((4, ROWS, BS), F32),
             pltpu.VMEM((4, ROWS, BS), F32),
             pltpu.SemaphoreType.DMA((N_SEM,)),
@@ -608,7 +620,7 @@
             collective_id=0, has_side_effects=True, vmem_limit_bytes=62 * 2**20
         ),
         name="shampoo",
-    )(owners, grads, roots_prev, moment_first, moment_second)
+    )(owners.T, grads, roots_prev, moment_first, moment_second)
     return pl.pallas_call(
         store,
         out_shape=(small, small, small, jax.ShapeDtypeStruct((1, 1, 2, BS, BS), BF16)),

time: 69.8 us -> 66.8 us (0.957)
  Pallas kernels: 67.7 us -> 66 us
  local copies, waits for them, and re-layouts: 1.32 us -> 0 us
    pallas_call x1, Pallas kernels: 65 us -> 63.3 us  [per_device(): pl.pallas_call(body, out_shape=(small, small, small, jax.ShapeDtypeStruct...]
    unnamed x1 -> x0, local copies, waits for them, and re-layouts: 1.32 us -> none
where the time goes in v3:
time: 66.8 us; the launch traced here: 66.6 us
  Pallas kernels  66 us (99%)
    pallas_call x1, Pallas kernels, per_device(): pl.pallas_call(body, out_shape=(small, small, small, jax.ShapeDtypeStruct...  63.3 us
    pallas_call x1, Pallas kernels, per_device(): pl.pallas_call(store, out_shape=(small, small, small, jax.ShapeDtypeStruc...  2.73 us

profile of v3, /device:TPU:1, one launch (start us, length us, event | category | flops | bytes accessed | tf_op | source)
XLA Modules:
  0.0 66.6 jit_solution(17652992094620716028)
XLA Ops:
  0.6 63.3 %shampoo.1 = (f32[4,32,512]{2,1,0:T(8,128)}, f32[4,32,512]{2,1,0:T(8,128)}, f32[4,32,512]{2,1,0:T(8,128)}, bf16[2,512,512]{2,1,0:T(8,128)(2,1)}) custom-call(s32[1,8]{1,0:T(1,128)} %bitcast.1, bf16[1,4,512,512]{3,2,1,0:T(8,128)(2,1)} %refs_1_.1, bf16[4,2,512,512]{3,2,1,0:T(8,128)(2,1)} %refs_2_.1, f32[4,32,512]{2,1,0:T(8,128)} %refs_3_.1, f32[4,32,512]{2,1,0:T(8,128)} %refs_4_.1), custom_call_target="tpu_custom_call" | custom-call | tf_op jit(solution)/shard_map/shampoo/pallas_call | solution.py:578
  63.9 2.7 %store.1 = (f32[4,32,512]{2,1,0:T(8,128)}, f32[4,32,512]{2,1,0:T(8,128)}, f32[4,32,512]{2,1,0:T(8,128)}, bf16[1,1,2,512,512]{4,3,2,1,0:T(8,128)(2,1)}) custom-call(f32[4,32,512]{2,1,0:T(8,128)} %get-tuple-element.8.u, f32[4,32,512]{2,1,0:T(8,128)} %get-tuple-element.9.a, f32[4,32,512]{2,1,0:T(8,128)} %get-tuple-element.10.b, ...), custom_call_target="tpu_custom_call" | custom-call | tf_op jit(solution)/shard_map/store/pallas_call | solution.py:624

commit v4 on v3

--- a/solution.py
+++ b/solution.py
@@ -155,7 +155,8 @@
                 RAW + 2 * n + h,
                 dev(x, 1 - y, cc),
             )
-            cp.start()
+            if n < 2:
+                cp.start()
             raw_cp.append(cp)
     sends += core_cp + raw_cp
 
@@ -251,6 +252,8 @@
     def grad_chunk(n):
         k = ORDER[n]
         g_send[k - 1] = raw_sum(n)
+        for cp in raw_cp[2 * (n + 2) : 2 * (n + 2) + 2]:
+            cp.start()
         cp = rc(g_send.at[k - 1], g_recv.at[k - 1], GRD + k - 1, GRD + k - 1, dev(xo(k), y, c))
         cp.start()
         grd_cp.append(cp)
@@ -414,6 +417,11 @@
         for k in (1, 3, 2):
             ring_cp(0, k).start()
 
+    for cp in sends + grd_cp:
+        cp.wait_send()
+    stat_sends(0, lambda cp: cp.wait_send())
+    stat_sends(1, lambda cp: cp.wait_send())
+
     for k in range(1, N_DP):
         gm_cp(k).wait_recv()
     loads[7].wait()
@@ -446,6 +454,9 @@
 
     for k in range(1, N_DP):
         s1_cp(k).start()
+    for k in range(1, N_DP):
+        gm_cp(k).wait_send()
+        sc_cp(k).wait_send()
 
     @pl.when(even)
     def _():
@@ -499,9 +510,9 @@
             return jnp.where(filled, pieces[idx, tile_of(n), :].astype(F32), 0.0)
 
         for n, (i, j) in enumerate(OFF_TILES):
-            t = piece_tile(n)
-            roots_new[slot, tile_of(i), tile_of(j)] = t.astype(BF16)
-            roots_new[slot, tile_of(j), tile_of(i)] = t.T.astype(BF16)
+            t = piece_tile(n).astype(BF16)
+            roots_new[slot, tile_of(i), tile_of(j)] = t
+            roots_new[slot, tile_of(j), tile_of(i)] = t.T
         dg = jnp.where(filled, pieces[idx, PIECE : PIECE + DIAG, :].astype(F32), 0.0)
         for n, (i, j) in ((6, (0, 1)), (7, (2, 3))):
             t = piece_tile(n)
@@ -522,11 +533,6 @@
     for b in range(4):
         update[b] = precond[b] * ratio
 
-    for cp in sends + grd_cp:
-        cp.wait_send()
-    stat_sends(0, lambda cp: cp.wait_send())
-    stat_sends(1, lambda cp: cp.wait_send())
-
     @pl.when(even)
     def _():
         for cp in y_cp:
@@ -545,8 +551,6 @@
         for s in range(2):
             sib_cp(row, s).wait_send()
     for k in range(1, N_DP):
-        gm_cp(k).wait_send()
-        sc_cp(k).wait_send()
         s1_cp(k).wait_send()
     for k in range(1, n_mp):
         s2_cp(k).wait_send()

time: 66.8 us -> 66.2 us (level)
  no operation moved by 1% of the time
where the time goes in v4:
time: 66.2 us; the launch traced here: 66.1 us
  Pallas kernels  65.5 us (99%)
    pallas_call x1, Pallas kernels, per_device(): pl.pallas_call(body, out_shape=(small, small, small, jax.ShapeDtypeStruct...  62.7 us
    pallas_call x1, Pallas kernels, per_device(): pl.pallas_call(store, out_shape=(small, small, small, jax.ShapeDtypeStruc...  2.73 us

profile of v4, /device:TPU:1, one launch (start us, length us, event | category | flops | bytes accessed | tf_op | source)
XLA Modules:
  0.0 66.1 jit_solution(9567578326181309114)
XLA Ops:
  0.6 62.7 %shampoo.1 = (f32[4,32,512]{2,1,0:T(8,128)}, f32[4,32,512]{2,1,0:T(8,128)}, f32[4,32,512]{2,1,0:T(8,128)}, bf16[2,512,512]{2,1,0:T(8,128)(2,1)}) custom-call(s32[1,8]{1,0:T(1,128)} %bitcast.1, bf16[1,4,512,512]{3,2,1,0:T(8,128)(2,1)} %refs_1_.1, bf16[4,2,512,512]{3,2,1,0:T(8,128)(2,1)} %refs_2_.1, f32[4,32,512]{2,1,0:T(8,128)} %refs_3_.1, f32[4,32,512]{2,1,0:T(8,128)} %refs_4_.1), custom_call_target="tpu_custom_call" | custom-call | tf_op jit(solution)/shard_map/shampoo/pallas_call | solution.py:582
  63.4 2.7 %store.1 = (f32[4,32,512]{2,1,0:T(8,128)}, f32[4,32,512]{2,1,0:T(8,128)}, f32[4,32,512]{2,1,0:T(8,128)}, bf16[1,1,2,512,512]{4,3,2,1,0:T(8,128)(2,1)}) custom-call(f32[4,32,512]{2,1,0:T(8,128)} %get-tuple-element.8.u, f32[4,32,512]{2,1,0:T(8,128)} %get-tuple-element.9.a, f32[4,32,512]{2,1,0:T(8,128)} %get-tuple-element.10.b, ...), custom_call_target="tpu_custom_call" | custom-call | tf_op jit(solution)/shard_map/store/pallas_call | solution.py:628
